TPU v7x, 1024 devices: a whole 4x4x32 slice. The times are simulated.
1024 devices in a mesh: grp: 64 (over z, core), loc: 16 (over x, y).
Axes of the slice: x: 4, y: 4, z: 32, core: 2. Of those that a mesh axis runs over, the one named last changes fastest.
Arguments:
- out_grad: bfloat16 [8192, 3584], P('grp', 'loc'), may hold values from -6 to 6
- group_choice: int32 [8192, 4], P('grp'), may hold values from 0 to 63, all different within a row; in each aligned block of 128 rows (0 to 127, 128 to 255, ...) at most 16 rows name the same one
- gate_weight: bfloat16 [8192, 4, 2], P('grp'), may hold values from 0.049804688 to 0.5
- gate_pre: bfloat16 [64, 1024, 2048], P('grp', None, 'loc'), may hold values from -6 to 6
- up_pre: bfloat16 [64, 1024, 2048], P('grp', None, 'loc'), may hold values from -6 to 6
- down_weight: bfloat16 [64, 2048, 3584], P('grp', None, 'loc'), may hold values from -0.1875 to 0.1875
- up_weight: bfloat16 [64, 2048, 3584], P('grp', None, 'loc'), may hold values from -0.1875 to 0.1875
Outputs:
- down_grad: bfloat16 [64, 2048, 3584], P('grp', None, 'loc')
- input_grad: bfloat16 [8192, 3584], P('grp', 'loc')
Inputs may be any that keep to these rules, and one draw needn't show every extreme that they name: `group_choice`: A token's 4 groups are distinct. Among the tokens of one index of grp (aligned blocks of 128 tokens) no group is chosen more than 16 times, a bound that some block reaches.
All inputs are finite; a program needn't handle non-finite values. Where the computation divides by a largest or mean magnitude, that divisor is 1e-20 or more.
Results may differ from a plain program's by a relative error of at most 0.023.
Values may be sent and summed in bfloat16 or wider, within the bound.
A program may use at most 64 MiB of HBM per device.

v0:
```python
import jax
import jax.numpy as jnp
from jax import lax
from jax.sharding import PartitionSpec as P


def on_device(out_grad, group_choice, gate_weight, gate_pre, up_pre, down_weight, up_weight):
    group_count = lax.axis_size("grp")
    tokens_here, feature_count = out_grad.shape
    pick_count = group_choice.shape[1]
    expert_count = gate_weight.shape[2]
    slot_count = gate_pre.shape[1]
    capacity = slot_count // group_count
    picked = (
        group_choice[:, :, None] == jnp.arange(group_count, dtype=jnp.int32)[None, None, :]
    ).astype(jnp.int32)
    group_load = jnp.sum(picked, axis=1)
    earlier = jnp.cumsum(group_load, axis=0) - group_load
    position = jnp.sum(picked * earlier[:, None, :], axis=2)
    slot_index = (group_choice * capacity + position).reshape(-1)
    chooser = slot_index[None, :] == jnp.arange(slot_count, dtype=jnp.int32)[:, None]
    token_map = jnp.sum(
        chooser.reshape(slot_count, tokens_here, pick_count).astype(jnp.int32), axis=2
    ).astype(jnp.bfloat16)
    outgoing = jnp.dot(token_map, out_grad, preferred_element_type=jnp.float32).astype(jnp.bfloat16)
    outgoing_gate = jnp.dot(
        chooser.astype(jnp.bfloat16),
        gate_weight.reshape(tokens_here * pick_count, expert_count),
        preferred_element_type=jnp.float32,
    ).astype(jnp.bfloat16)
    arrived, arrived_gate = (
        lax.all_to_all(
            outgoing.reshape(group_count, capacity, feature_count),
            "grp",
            split_axis=0,
            concat_axis=0,
            tiled=True,
        ),
        lax.all_to_all(
            outgoing_gate.reshape(group_count, capacity, expert_count),
            "grp",
            split_axis=0,
            concat_axis=0,
            tiled=True,
        ),
    )
    arrived = arrived.reshape(slot_count, feature_count)
    arrived_gate = arrived_gate.reshape(slot_count, expert_count)
    weighted = (
        arrived_gate.astype(jnp.float32)[:, :, None] * arrived.astype(jnp.float32)[:, None, :]
    )
    weighted_bf = weighted.astype(jnp.bfloat16)
    down_block = down_weight[0].reshape(expert_count, -1, feature_count)
    partial_value = jnp.einsum(
        "red,efd->ref", weighted_bf, down_block, preferred_element_type=jnp.float32
    ).reshape(slot_count, -1)
    hidden_grad = lax.psum_scatter(
        partial_value.astype(jnp.bfloat16), "loc", scatter_dimension=1, tiled=True
    ).astype(jnp.float32)
    activation = jax.nn.silu(gate_pre[0].astype(jnp.float32))
    hidden = (activation * up_pre[0].astype(jnp.float32)).astype(jnp.bfloat16)
    up_grad = (hidden_grad * activation).astype(jnp.bfloat16)
    hidden_all, up_grad_all = (
        lax.all_gather(hidden, "loc", axis=1, tiled=True),
        lax.all_gather(up_grad, "loc", axis=1, tiled=True),
    )
    column_scale = jnp.max(jnp.abs(weighted), axis=0) + 1e-06
    quantized = (weighted / column_scale[None, :, :]).astype(jnp.bfloat16)
    weight_grad = jnp.einsum(
        "ref,red->efd",
        hidden_all.reshape(slot_count, expert_count, -1),
        quantized,
        preferred_element_type=jnp.float32,
    )
    down_grad = (
        (weight_grad * column_scale[:, None, :]).astype(jnp.bfloat16).reshape(1, -1, feature_count)
    )
    returning = jnp.dot(up_grad_all, up_weight[0], preferred_element_type=jnp.float32).astype(
        jnp.bfloat16
    )
    returned = lax.all_to_all(
        returning.reshape(group_count, capacity, feature_count),
        "grp",
        split_axis=0,
        concat_axis=0,
        tiled=True,
    )
    returned = returned.reshape(slot_count, feature_count)
    input_grad = lax.dot_general(
        token_map, returned, (((0,), (0,)), ((), ())), preferred_element_type=jnp.float32
    ).astype(jnp.bfloat16)
    return (down_grad, input_grad)


def solution(mesh):
    return jax.shard_map(
        on_device,
        mesh=mesh,
        in_specs=(
            P("grp", "loc"),
            P("grp", None),
            P("grp", None, None),
            P("grp", None, "loc"),
            P("grp", None, "loc"),
            P("grp", None, "loc"),
            P("grp", None, "loc"),
        ),
        out_specs=(P("grp", None, "loc"), P("grp", "loc")),
        check_vma=False,
    )
```

profile of v0, /device:TPU:1, one launch (start us, length us, event | category | flops | bytes accessed | tf_op | source)
XLA Modules:
  0.0 434.5 jit_solution(17397811241863295872)
XLA Ops:
  7.2 0.0 copy-start
  7.2 0.0 copy-start.4
  7.2 0.8 convert_reduce_fusion.1
  8.0 0.1 copy.56
  8.1 0.2 reduce_window_sum.11
  8.3 0.1 copy.58
  8.3 0.7 select_reduce_fusion
  9.1 0.7 multiply_add_fusion
  9.8 0.1 copy.59
  9.9 0.1 eq.38
  10.0 0.8 copy.60
  10.8 0.1 reshape.74
  10.9 0.0 copy-start.1
  11.0 0.5 fusion.3
  11.4 0.1 reshape.75
  11.5 0.7 copy.61
  12.2 30.4 %all-to-all-start = ((bf16[64,16,2]{1,2,0:T(2,128)(2,1)}), bf16[64,16,2]{1,2,0:T(2,128)(2,1)S(1)}, u32[]{:S(2)}, u32[]{:S(2)}) async-start(bf16[64,16,2]{1,2,0:T(2,128)(2,1)} %copy.61), calls=%async_computation | async-start | bytes 65536 | tf_op jit(solution)/shard_map/all_to_all | solution.py:39
  42.6 0.3 convert_reduce_fusion
  42.8 0.0 copy-done.4
  42.8 0.3 convolution_convert_fusion.2
  43.1 1.0 copy.64
  44.1 20.8 %all-to-all-done = bf16[64,16,2]{1,2,0:T(2,128)(2,1)S(1)} async-done(((bf16[64,16,2]{1,2,0:T(2,128)(2,1)}), bf16[64,16,2]{1,2,0:T(2,128)(2,1)S(1)}, u32[]{:S(2)}, u32[]{:S(2)}) %all-to-all-start) | async-done | bytes 4128 | tf_op jit(solution)/shard_map/all_to_all | solution.py:39
  64.9 5.7 %all-to-all-start.1 = ((bf16[64,16,224]{2,1,0:T(8,128)(2,1)}), bf16[64,16,224]{2,1,0:T(8,128)(2,1)S(1)}, u32[]{:S(2)}, u32[]{:S(2)}) async-start(bf16[64,16,224]{2,1,0:T(8,128)(2,1)} %bitcast.4), calls=%async_computation.1 | async-start | bytes 1048576 | tf_op jit(solution)/shard_map/all_to_all | solution.py:32
  70.6 0.0 reduce-scatter.2.cloned.1.call-start
  70.6 0.0 copy-done.1
  70.6 1.6 reshape_squeeze.3
  72.2 0.1 copy.62
  72.3 0.1 copy.63
  72.4 0.1 reshape.82
  72.5 62.5 %all-to-all-done.1 = bf16[64,16,224]{2,1,0:T(8,128)(2,1)S(1)} async-done(((bf16[64,16,224]{2,1,0:T(8,128)(2,1)}), bf16[64,16,224]{2,1,0:T(8,128)(2,1)S(1)}, u32[]{:S(2)}, u32[]{:S(2)}) %all-to-all-start.1) | async-done | bytes 458784 | tf_op jit(solution)/shard_map/all_to_all | solution.py:32
  135.0 0.1 bitcast_convert_fusion
  135.1 0.3 copy.65
  135.4 4.5 %convolution_convert_fusion = bf16[2,1024,1024]{1,2,0:T(8,128)(2,1)} fusion(bf16[2,1024,224]{1,0,2:T(2,128)(2,1)} %reshape_squeeze.3, f32[1024,224]{0,1:T(8,128)S(1)} %copy.65, f32[1024,2]{0,1:T(2,128)S(1)} %reshape.82), kind=kOutput, calls=%fused_computation.3 | convolution fusion | flops 942538752 | bytes 6037504 | tf_op jit(solution)/shard_map/red,efd->ref/dot_general | solution.py:54
  139.9 0.0 copy-start.2
  139.9 0.0 copy-start.3
  139.9 0.0 reduce-scatter.2.cloned.1.call-update
  139.9 0.0 all-gather.5.cloned.1.call-start
  140.0 0.9 copy-done.2
  140.9 0.1 copy.54
  141.0 0.0 copy-done.3
  141.0 0.1 copy.55
  141.2 92.9 %reduce-scatter.2.cloned.1.call-done = bf16[1024,128]{0,1:T(8,128)(2,1)} async-done(((bf16[1024,2048]{0,1:T(8,128)(2,1)}), bf16[1024,128]{0,1:T(8,128)(2,1)}) %reduce-scatter.2.cloned.1.call-update) | async-done | bytes 262160 | tf_op jit(solution)/shard_map/reduce_scatter | solution.py:57
  234.1 2.0 multiply_convert_fusion.3
  236.2 0.0 all-gather.5.cloned.1.call-update
  236.2 0.0 all-gather.3.cloned.1.call-start
  236.2 0.7 all-gather.3.cloned.1.call-update
  236.9 91.5 %all-gather.5.cloned.1.call-done = bf16[1024,2048]{0,1:T(8,128)(2,1)} async-done(((bf16[1024,128]{0,1:T(8,128)(2,1)}), bf16[1024,2048]{0,1:T(8,128)(2,1)}) %all-gather.5.cloned.1.call-update) | async-done | bytes 4194320 | tf_op jit(solution)/shard_map/all_gather | solution.py:65
  328.5 0.0 copy-done
  328.5 3.3 convolution_convert_fusion.1
  331.8 1.0 copy.69
  332.8 23.8 %all-to-all-start.2 = ((bf16[64,16,224]{2,1,0:T(8,128)(2,1)}), bf16[64,16,224]{2,1,0:T(8,128)(2,1)S(1)}, u32[]{:S(2)}, u32[]{:S(2)}) async-start(bf16[64,16,224]{2,1,0:T(8,128)(2,1)} %bitcast.9), calls=%async_computation.3 | async-start | bytes 1048576 | tf_op jit(solution)/shard_map/all_to_all | solution.py:81
  356.5 0.3 fusion.2
  356.8 63.9 %all-gather.3.cloned.1.call-done = bf16[1024,2048]{0,1:T(8,128)(2,1)} async-done(((bf16[1024,128]{0,1:T(8,128)(2,1)}), bf16[1024,2048]{0,1:T(8,128)(2,1)}) %all-gather.3.cloned.1.call-update) | async-done | bytes 4194320 | tf_op jit(solution)/shard_map/all_gather | solution.py:64
  420.7 3.7 multiply_convert_fusion.1
  424.5 0.9 copy.67
  425.4 1.6 reshape.77
  427.0 0.0 all-to-all-done.2
  427.0 1.0 convolution_convert_fusion.3
  (2 shorter events, 0.0 us)
Async XLA Ops:
  7.2 321.3 %copy-start = (bf16[1,2048,224]{1,2,0:T(8,128)(2,1)S(1)}, bf16[1,2048,224]{1,2,0:T(8,128)(2,1)}, u32[]{:S(2)}) copy-start(bf16[1,2048,224]{1,2,0:T(8,128)(2,1)} %param.13) | copy-start | bytes 2752516
  7.2 35.6 %copy-start.4 = (bf16[128,224]{0,1:T(8,128)(2,1)S(1)}, bf16[128,224]{0,1:T(8,128)(2,1)}, u32[]{:S(2)}) copy-start(bf16[128,224]{0,1:T(8,128)(2,1)} %param.7) | copy-start | bytes 172036
  10.9 59.7 %copy-start.1 = (bf16[1,2048,224]{1,2,0:T(8,128)(2,1)S(1)}, bf16[1,2048,224]{1,2,0:T(8,128)(2,1)}, u32[]{:S(2)}) copy-start(bf16[1,2048,224]{1,2,0:T(8,128)(2,1)} %param.12) | copy-start | bytes 2752516
  12.2 52.8 %all-to-all-start = ((bf16[64,16,2]{1,2,0:T(2,128)(2,1)}), bf16[64,16,2]{1,2,0:T(2,128)(2,1)S(1)}, u32[]{:S(2)}, u32[]{:S(2)}) async-start(bf16[64,16,2]{1,2,0:T(2,128)(2,1)} %copy.61), calls=%async_computation | async-start | bytes 65536 | tf_op jit(solution)/shard_map/all_to_all | solution.py:39
  64.9 70.1 %all-to-all-start.1 = ((bf16[64,16,224]{2,1,0:T(8,128)(2,1)}), bf16[64,16,224]{2,1,0:T(8,128)(2,1)S(1)}, u32[]{:S(2)}, u32[]{:S(2)}) async-start(bf16[64,16,224]{2,1,0:T(8,128)(2,1)} %bitcast.4), calls=%async_computation.1 | async-start | bytes 1048576 | tf_op jit(solution)/shard_map/all_to_all | solution.py:32
  70.6 163.5 %reduce-scatter.2.cloned.1.call-start = ((), (), s32[]{:S(2)}) async-start(), calls=%async_computation.5 | async-start | bytes 4456448 | tf_op jit(solution)/shard_map/reduce_scatter | solution.py:57
  139.9 0.9 copy-start.2
  139.9 1.1 copy-start.3
  139.9 188.5 %all-gather.5.cloned.1.call-start = ((), (), s32[]{:S(2)}) async-start(), calls=%async_computation.6 | async-start | bytes 4456448 | tf_op jit(solution)/shard_map/all_gather | solution.py:65
  236.2 184.5 %all-gather.3.cloned.1.call-start = ((), (), s32[]{:S(2)}) async-start(), calls=%async_computation.4 | async-start | bytes 4456448 | tf_op jit(solution)/shard_map/all_gather | solution.py:64
  332.8 94.3 %all-to-all-start.2 = ((bf16[64,16,224]{2,1,0:T(8,128)(2,1)}), bf16[64,16,224]{2,1,0:T(8,128)(2,1)S(1)}, u32[]{:S(2)}, u32[]{:S(2)}) async-start(bf16[64,16,224]{2,1,0:T(8,128)(2,1)} %bitcast.9), calls=%async_computation.3 | async-start | bytes 1048576 | tf_op jit(solution)/shard_map/all_to_all | solution.py:81
Sparse Core Ops, SparseCore 0:
  140.1 94.0 reduce-scatter.1
  239.6 88.8 all-gather.4
  333.4 87.3 all-gather.2
where the time goes:
time: 435 us
  waiting for transfers between devices  332 us (76%)
  starting transfers between devices  60 us (14%)
  between operations  13.9 us (3%)
  matrix products  13.2 us (3%)
  local copies, waits for them, and re-layouts  10 us (2%)
  other arithmetic  5.06 us (1%)
    reduce_scatter x1, waiting for transfers between devices, on_device(): lax.psum_scatter(partial_value.astype(jnp.bfloat16), 'loc', scatter_dimen...  92.9 us
    all_gather x1, waiting for transfers between devices, on_device(): lax.all_gather(up_grad, 'loc', axis=1, tiled=True)  91.5 us
    all_gather x1, waiting for transfers between devices, on_device(): lax.all_gather(hidden, 'loc', axis=1, tiled=True)  63.9 us
    all_to_all x1, waiting for transfers between devices, on_device(): lax.all_to_all(outgoing.reshape(group_count, capacity, feature_count), 'g...  62.5 us
    all_to_all x1, starting transfers between devices, on_device(): lax.all_to_all(outgoing_gate.reshape(group_count, capacity, expert_count)...  30.4 us
    all_to_all x1, starting transfers between devices, on_device(): lax.all_to_all(returning.reshape(group_count, capacity, feature_count), '...  23.8 us
    all_to_all x1, waiting for transfers between devices, on_device(): lax.all_to_all(outgoing_gate.reshape(group_count, capacity, expert_count)...  20.8 us
  transfers between devices with their start and end apart: 6, of which 5 were waited for; matrix products, arithmetic and copies ran while one was open for 3% of the time, Pallas kernels for 0%

commit v1 on v0

v1 whole, which is shorter than its diff:
```python
import functools

import jax
import jax.numpy as jnp
from jax import lax
from jax.experimental import pallas as pl
from jax.experimental.pallas import tpu as pltpu
from jax.sharding import PartitionSpec as P

MESH = pl.DeviceIdType.MESH
NT = (((1,), (1,)), ((), ()))
TN = (((0,), (0,)), ((), ()))
F32 = jnp.float32
BF16 = jnp.bfloat16
ZP = 3
RP = 2


def moe_kernel(
    x_ref, choice_ref, gates_ref, gp_ref, up_ref, wd_ref, wu_ref,
    dg_ref, ig_ref,
    allx, wf, wbf, wt, qt, cst, act, gh0, gh1, gu0, gu1, pa0, pa1, op0, op1, ma0, ma1,
    s10, s11, op20, op21, ma20, ma21, ret, own, sibs, sibr, ringr, rings,
    zsend, zrecv, bsend, brecv, xsend, xrecv, rsend, rrecv, csend, crecv,
):
    n_grp = allx.shape[0]
    n_z = n_grp // 2
    half = n_z // 2
    feats, toks = x_ref.shape
    meta_rows = allx.shape[1] - feats
    slots = gp_ref.shape[0]
    cap = slots // n_grp
    hw = gp_ref.shape[1]
    hs = slots // 2
    qs = hs // 2
    picks = choice_ref.shape[0]
    per_e = 8

    g = lax.axis_index("grp")
    loc = lax.axis_index("loc")
    z, c = lax.div(g, 2), lax.rem(g, 2)
    x, y = lax.div(loc, 4), lax.rem(loc, 4)
    gz = lambda r: lax.rem(z + r + 2 * n_z, n_z)
    zdev = [(gz(1) * 2 + c, loc), (gz(-1) * 2 + c, loc)]
    sib = (z * 2 + 1 - c, loc)
    xdev = [(g, lax.rem(x + 1, 4) * 4 + y), (g, lax.rem(x + 3, 4) * 4 + y)]
    ydev = [(g, x * 4 + lax.rem(y + 1, 4)), (g, x * 4 + lax.rem(y + 3, 4))]
    pos1, pos2 = [x, y], [y, x]
    dev1, dev2 = [xdev, ydev], [ydev, xdev]
    gh, gu, part = [gh0, gh1], [gu0, gu1], [pa0, pa1]
    opp, main = [op0, op1], [ma0, ma1]
    s1, opp2, main2 = [s10, s11], [op20, op21], [ma20, ma21]

    def copy(src, dst, ss, rs, dev):
        return pltpu.make_async_remote_copy(
            src_ref=src, dst_ref=dst, send_sem=ss, recv_sem=rs, device_id=dev, device_id_type=MESH
        )

    barrier = pltpu.get_barrier_semaphore()
    for dev in zdev + [sib] + xdev + ydev:
        pl.semaphore_signal(barrier, inc=1, device_id=dev, device_id_type=MESH)

    choice = choice_ref[...].astype(F32)
    ids = lax.broadcasted_iota(jnp.int32, (n_grp, toks), 0).astype(F32)
    hits = [choice[k : k + 1] == ids for k in range(picks)]
    load = sum(h.astype(F32) for h in hits).astype(BF16)
    before = (
        lax.broadcasted_iota(jnp.int32, (toks, toks), 0) < lax.broadcasted_iota(jnp.int32, (toks, toks), 1)
    ).astype(F32).astype(BF16)
    earlier = jnp.dot(load, before, preferred_element_type=F32)
    row8 = lax.broadcasted_iota(jnp.int32, (8, toks), 0)
    low = jnp.zeros((8, toks), F32)
    for k in range(picks):
        place = jnp.sum(jnp.where(hits[k], earlier, 0.0), axis=0, keepdims=True)
        low = jnp.where(row8 == k, choice[k : k + 1], low)
        low = jnp.where(row8 == picks + k, place, low)
    meta = jnp.concatenate([gates_ref[...].astype(F32), low], axis=0)
    allx[g, 0:feats, :] = x_ref[...]
    allx[g, feats:, :] = meta.astype(BF16)

    pl.semaphore_wait(barrier, 7)

    zrows = allx.shape[1] // ZP

    def blk(r):
        return gz(r) * 2 + c

    def zcopy(d, s, p):
        ref = allx.at[blk(-s if d == 0 else s), pl.ds(p * zrows, zrows), :]
        return copy(ref, ref, zsend.at[d, s, p], zrecv.at[d, s, p], zdev[d])

    def zwait(d, s, p):
        ref = allx.at[blk(-(s + 1) if d == 0 else s + 1), pl.ds(p * zrows, zrows), :]
        copy(ref, ref, zsend.at[d, s, p], zrecv.at[d, s, p], zdev[d]).wait_recv()

    def bcopy(d, s):
        ref = allx.at[blk(-s if d == 0 else s)]
        return copy(ref, ref, bsend.at[d, s], brecv.at[d, s], sib)

    def bwait(d, s):
        ref = allx.at[gz(-s if d == 0 else s) * 2 + 1 - c]
        copy(ref, ref, bsend.at[d, s], brecv.at[d, s], sib).wait_recv()

    gf = g.astype(F32)

    def chosen(i):
        m = allx[i, feats:, :].astype(F32)
        place = jnp.full((1, toks), -1.0, F32)
        gate = [jnp.zeros((1, toks), F32), jnp.zeros((1, toks), F32)]
        for k in range(picks):
            sel = m[8 + k : 9 + k] == gf
            place = jnp.where(sel, m[8 + picks + k : 9 + picks + k], place)
            for e in range(2):
                gate[e] = jnp.where(sel, m[2 * k + e : 2 * k + e + 1], gate[e])
        hit = lax.broadcasted_iota(jnp.int32, (cap, toks), 0).astype(F32) == place
        return hit, gate

    def build(i):
        hit, gate = chosen(i)
        lhs = jnp.concatenate([jnp.where(hit, gate[0], 0.0), jnp.where(hit, gate[1], 0.0)], axis=0).astype(BF16)
        w = lax.dot_general(lhs, allx[i, 0:feats, :], NT, preferred_element_type=F32)
        at = pl.ds(pl.multiple_of(i * cap, cap), cap)
        for e in range(2):
            wf[e, at, 0:feats] = w[e * cap : (e + 1) * cap]
            wbf[e, at, 0:feats] = w[e * cap : (e + 1) * cap].astype(BF16)

    def zstep(s, up=True, down=True, lag=True):
        for p in range(ZP):
            zwait(0, s - 1, p)
            if up:
                zcopy(0, s, p).start()
            if down is not None:
                zwait(1, s - 1, p)
                if down:
                    zcopy(1, s, p).start()
        bcopy(0, s).start()
        build(blk(-s))
        if down is not None:
            bcopy(1, s).start()
            build(blk(s))
        if lag:
            for d in range(2):
                bwait(d, s - 1)
                build(gz(-(s - 1) if d == 0 else s - 1) * 2 + 1 - c)

    def zloop(lo, hi):
        lo, hi = min(lo, half - 1), min(hi, half - 1)
        if lo < hi:
            def step(s, carry):
                zstep(s)
                return carry
            lax.fori_loop(lo, hi, step, 0)

    def ring(stage, h):
        a = (pos1 if stage in (0, 3, 5) else pos2)[h]
        dev = (dev1 if stage in (0, 3, 5) else dev2)[h]
        nxt = [lax.rem(a + 1, 4), lax.rem(a + 3, 4)]
        return a, dev, nxt, lax.rem(a + 2, 4)

    def xcopy(stage, h, side, n, src, dst):
        _, dev, _, _ = ring(stage, h)
        return copy(src, dst, xsend.at[stage, h, side, n], xrecv.at[stage, h, side, n], dev[side])

    def rs_refs(stage, h):
        return (part[h], opp[h], main[h]) if stage == 0 else (s1[h], opp2[h], main2[h])

    def rs_copy(stage, h, side, n):
        _, _, nxt, far = ring(stage, h)
        src, o, m = rs_refs(stage, h)
        if n == 0:
            return xcopy(stage, h, side, 0, src.at[far, side], o.at[side])
        if n == 1:
            return xcopy(stage, h, side, 1, src.at[nxt[side], 1 - side], m.at[side, 1 - side])
        return xcopy(stage, h, side, 2, src.at[nxt[side], side], m.at[side, side])

    def rs_add(stage, h, side):
        _, _, nxt, _ = ring(stage, h)
        src, o, _ = rs_refs(stage, h)
        rs_copy(stage, h, side, 0).wait_recv()
        rows = src.shape[2]
        piece = min(rows, 128)

        def step(q, carry):
            at = pl.ds(pl.multiple_of(q * piece, piece), piece)
            total = src[nxt[side], side, at, :].astype(F32) + o[side, at, :].astype(F32)
            src[nxt[side], side, at, :] = total.astype(BF16)
            return carry

        lax.fori_loop(0, rows // piece, step, 0)
        rs_copy(stage, h, side, 2).start()

    def rs_wait_main(stage, h):
        for side in range(2):
            rs_copy(stage, h, side, 1).wait_recv()
            rs_copy(stage, h, side, 2).wait_recv()

    def ag_ref(stage, store, h, who, k):
        if stage in (3, 5):
            return store[h].at[who, k]
        a = pos1[h]
        return store[h].at[a, lax.div(who, 2), pl.ds(pl.multiple_of(lax.rem(who, 2) * hs + k * qs, qs), qs), :]

    def ag_copy(stage, store, h, side, n):
        a, _, nxt, _ = ring(stage, h)
        if n == 2:
            ref = ag_ref(stage, store, h, nxt[1 - side], side)
        else:
            ref = ag_ref(stage, store, h, a, side if n == 0 else 1 - side)
        return xcopy(stage, h, side, n, ref, ref)

    def ag_wait(stage, store, h, side, n):
        _, _, nxt, far = ring(stage, h)
        if n == 2:
            ref = ag_ref(stage, store, h, far, side)
        else:
            ref = ag_ref(stage, store, h, nxt[1 - side], side if n == 0 else 1 - side)
        xcopy(stage, h, side, n, ref, ref).wait_recv()

    def ag_send(stage, store, h):
        for n in range(2):
            for side in range(2):
                ag_copy(stage, store, h, side, n).start()

    def ag_pass(stage, store, h):
        for side in range(2):
            ag_wait(stage, store, h, side, 0)
            ag_copy(stage, store, h, side, 2).start()

    def ag_finish(stage, store, h):
        for side in range(2):
            ag_wait(stage, store, h, side, 1)
            ag_wait(stage, store, h, side, 2)

    def own_rows(h, k):
        return (pos1[h], lax.div(pos2[h], 2), pl.ds(pl.multiple_of(lax.rem(pos2[h], 2) * hs + k * qs, qs), qs))

    for p in range(ZP):
        for d in range(2):
            zcopy(d, 0, p).start()
    bcopy(0, 0).start()

    for h in range(2):
        for k in range(2):
            at = pl.ds(h * hs + k * qs, qs)
            v = gp_ref[at, :].astype(F32)
            a = v / (1.0 + jnp.exp(-v))
            act[at, :] = a
            i0, i1, i2 = own_rows(h, k)
            gh[h][i0, i1, i2, :] = (a * up_ref[at, :].astype(F32)).astype(BF16)
    for h in range(2):
        ag_send(2, gh, h)
    build(g)
    bwait(0, 0)
    build(z * 2 + 1 - c)

    zstep(1, down=half > 2, lag=False)
    zloop(2, 4)
    for h in range(2):
        ag_pass(2, gh, h)
    zloop(4, 6)
    for h in range(2):
        ag_finish(2, gh, h)
        ag_send(3, gh, h)
    zloop(6, 12)
    for h in range(2):
        ag_pass(3, gh, h)
    zloop(12, half - 1)
    if half > 2:
        zstep(half - 1, down=False)
    zstep(half, up=False, down=None)
    bwait(0, half)
    build(gz(-half) * 2 + 1 - c)

    def partial(h, t):
        def step(q, carry):
            b = lax.div(q, 2)
            l = t * 4 + b if h == 0 else b * 4 + t
            rows = pl.ds(pl.multiple_of(h * hs + lax.rem(q, 2) * qs, qs), qs)
            v = jnp.dot(
                wbf[lax.div(l, per_e), rows, 0:feats],
                wd_ref[:, pl.ds(pl.multiple_of(l * hw, hw), hw)],
                preferred_element_type=F32,
            )
            part[h][t, lax.div(q, 4), pl.ds(pl.multiple_of(lax.rem(q, 4) * qs, qs), qs), :] = v.astype(BF16)
            return carry

        lax.fori_loop(0, 8, step, 0)

    for h in range(2):
        partial(h, ring(0, h)[3])
        for side in range(2):
            rs_copy(0, h, side, 0).start()
    for side in range(2):
        for h in range(2):
            partial(h, ring(0, h)[2][side])
            rs_copy(0, h, side, 1).start()
    for h in range(2):
        for side in range(2):
            rs_add(0, h, side)
    for h in range(2):
        partial(h, ring(0, h)[0])

    def turn(q, carry):
        at = pl.ds(pl.multiple_of(q * 128, 128), 128)
        for e in range(2):
            for k in range(0, wf.shape[2], 128):
                wt[e, k : k + 128, at] = wf[e, at, k : k + 128].T
        return carry

    lax.fori_loop(0, slots // 128, turn, 0)
    for e in range(2):
        top = jnp.max(jnp.abs(wt[e, 0:feats, :]), axis=1, keepdims=True) + 1e-6
        cst[e] = jnp.broadcast_to(top, (feats, 128))

    def scale(q, carry):
        at = pl.ds(pl.multiple_of(q * 128, 128), 128)
        for e in range(2):
            qt[e, :, at] = (wt[e, 0:feats, at] / cst[e]).astype(BF16)
        return carry

    lax.fori_loop(0, slots // 128, scale, 0)

    for h in range(2):
        rs_wait_main(0, h)

        def add1(q, carry):
            k = lax.div(q, 4)
            at = pl.ds(pl.multiple_of(lax.rem(q, 4) * qs, qs), qs)
            total = (
                part[h][pos1[h], k, at, :].astype(F32)
                + main[h][0, k, at, :].astype(F32)
                + main[h][1, k, at, :].astype(F32)
            )
            s1[h][lax.div(q, 2), lax.rem(q, 2)] = total.astype(BF16)
            return carry

        lax.fori_loop(0, 8, add1, 0)
        for side in range(2):
            rs_copy(1, h, side, 0).start()
            rs_copy(1, h, side, 1).start()
    for h in range(2):
        for side in range(2):
            rs_add(1, h, side)
    for h in range(2):
        ag_finish(3, gh, h)
    for h in range(2):
        rs_wait_main(1, h)
        for k in range(2):
            at = pl.ds(h * hs + k * qs, qs)
            total = (
                s1[h][pos2[h], k].astype(F32) + main2[h][0, k].astype(F32) + main2[h][1, k].astype(F32)
            )
            i0, i1, i2 = own_rows(h, k)
            gu[h][i0, i1, i2, :] = (total * act[at, :]).astype(BF16)
        ag_send(4, gu, h)
    for h in range(2):
        ag_pass(4, gu, h)
    for h in range(2):
        ag_finish(4, gu, h)
        ag_send(5, gu, h)

    def grad(q, carry):
        e = lax.div(q, per_e)
        xx, yy = lax.div(q, 4), lax.rem(q, 4)
        at = pl.ds(pl.multiple_of(q * hw, hw), hw)
        total = jnp.zeros((feats, hw), F32)
        for h, (i, j) in enumerate(((xx, yy), (yy, xx))):
            hid = gh[h][i, lax.div(j, 2), pl.ds(pl.multiple_of(lax.rem(j, 2) * hs, hs), hs), :]
            total += jnp.dot(qt[e, :, h * hs : (h + 1) * hs], hid, preferred_element_type=F32)
        dg_ref[:, at] = (total * cst[e]).astype(BF16)
        return carry

    lax.fori_loop(0, 8, grad, 0)
    for h in range(2):
        ag_pass(5, gu, h)
    lax.fori_loop(8, 16, grad, 0)
    for h in range(2):
        ag_finish(5, gu, h)

        def back(q, carry):
            total = jnp.zeros((qs, feats), F32)
            for i in range(4):
                for j in range(4):
                    l = i * 4 + j if h == 0 else j * 4 + i
                    up = gu[h][i, j // 2, pl.ds(pl.multiple_of((j % 2) * hs + q * qs, qs), qs), :]
                    total += lax.dot_general(up, wu_ref[:, l * hw : (l + 1) * hw], NT, preferred_element_type=F32)
            ret[pl.ds(pl.multiple_of(h * hs + q * qs, qs), qs), 0:feats] = total.astype(BF16)
            return carry

        lax.fori_loop(0, 2, back, 0)

    rrows = feats // RP

    def contrib(n):
        zt = gz(n)
        i, j = zt * 2 + c, zt * 2 + 1 - c
        rows = jnp.concatenate(
            [
                ret[pl.ds(pl.multiple_of(i * cap, cap), cap), 0:feats],
                ret[pl.ds(pl.multiple_of(j * cap, cap), cap), 0:feats],
            ],
            axis=0,
        )
        mine, other = chosen(i)[0].astype(F32), chosen(j)[0].astype(F32)
        none = jnp.zeros((cap, toks), F32)
        pick = jnp.concatenate(
            [jnp.concatenate([mine, none], axis=1), jnp.concatenate([none, other], axis=1)], axis=0
        ).astype(BF16)
        v = lax.dot_general(rows, pick, TN, preferred_element_type=F32).astype(BF16)
        own[n] = v[:, 0:toks]
        sibs[n] = v[:, toks:]
        copy(sibs.at[n], sibr.at[n], csend.at[n], crecv.at[n], sib).start()

    def cwait(n):
        copy(sibs.at[n], sibr.at[n], csend.at[n], crecv.at[n], sib).wait_recv()

    def index(d, s):
        return half - s if d == 0 else lax.rem(half + 1 + s, n_z)

    def rcopy(d, s, p):
        at = pl.ds(p * rrows, rrows)
        return copy(rings.at[d, s, at, :], ringr.at[d, s, at, :], rsend.at[d, s, p], rrecv.at[d, s, p], zdev[d])

    def rstep(s, first=False, both=True):
        dirs = (0, 1) if both else (0,)
        for d in dirs:
            cwait(index(d, s))
        for p in range(RP):
            at = slice(p * rrows, (p + 1) * rrows)
            for d in dirs:
                n = index(d, s)
                total = own[n, at, :].astype(F32) + sibr[n, at, :].astype(F32)
                if not first:
                    rcopy(d, s - 1, p).wait_recv()
                    total += ringr[d, s - 1, at, :].astype(F32)
                rings[d, s, at, :] = total.astype(BF16)
                rcopy(d, s, p).start()

    contrib(index(0, 0))
    contrib(index(1, 0))
    contrib(index(0, 1))
    contrib(index(1, 1))
    rstep(0, first=True)

    def rloop(s, carry):
        contrib(index(0, s + 1))
        contrib(index(1, s + 1))
        rstep(s)
        return carry

    lax.fori_loop(1, half - 1, rloop, 0)
    rstep(half - 1, both=False)
    cwait(0)
    for p in range(RP):
        at = slice(p * rrows, (p + 1) * rrows)
        rcopy(0, half - 1, p).wait_recv()
        rcopy(1, half - 2, p).wait_recv()
        ig_ref[at, :] = (
            own[0, at, :].astype(F32)
            + sibr[0, at, :].astype(F32)
            + ringr[0, half - 1, at, :].astype(F32)
            + ringr[1, half - 2, at, :].astype(F32)
        ).astype(BF16)

    def drain(lo, hi, what):
        def step(s, carry):
            what(s)
            return carry
        lax.fori_loop(lo, hi, step, 0)

    for d in range(2):
        for p in range(ZP):
            drain(0, half - d, lambda s: zcopy(d, s, p).wait_send())
        for p in range(RP):
            drain(0, half - d, lambda s: rcopy(d, s, p).wait_send())
    drain(0, half + 1, lambda s: bcopy(0, s).wait_send())
    drain(1, half, lambda s: bcopy(1, s).wait_send())
    drain(0, n_z, lambda n: copy(sibs.at[n], sibr.at[n], csend.at[n], crecv.at[n], sib).wait_send())
    for h in range(2):
        for side in range(2):
            for n in range(3):
                for stage in (0, 1):
                    rs_copy(stage, h, side, n).wait_send()
                for stage, store in ((2, gh), (3, gh), (4, gu), (5, gu)):
                    ag_copy(stage, store, h, side, n).wait_send()


def on_device(out_grad, group_choice, gate_weight, gate_pre, up_pre, down_weight, up_weight):
    n_grp = lax.axis_size("grp")
    half = n_grp // 4
    toks, feats = out_grad.shape
    picks, experts = gate_weight.shape[1:]
    slots, hw = gate_pre.shape[1:]
    hidden = down_weight.shape[1]
    hs, qs = slots // 2, slots // 4
    wide = -(-feats // 128) * 128
    vm = lambda shape, kind=BF16: pltpu.VMEM(shape, kind)
    sem = lambda *shape: pltpu.SemaphoreType.DMA(shape)
    meta = picks * (experts + 2)
    scratch = [
        vm((n_grp, feats + meta, toks)),
        vm((experts, slots, wide), F32), vm((experts, slots, wide)),
        vm((experts, wide, slots), F32), vm((experts, feats, slots)), vm((experts, feats, 128), F32),
        vm((slots, hw), F32),
        *[vm((4, 2, 2 * hs, hw)) for _ in range(6)],
        *[vm((2, 2 * hs, hw)) for _ in range(2)],
        *[vm((2, 2, 2 * hs, hw)) for _ in range(2)],
        *[vm((4, 2, qs, hw)) for _ in range(2)],
        *[vm((2, qs, hw)) for _ in range(2)],
        *[vm((2, 2, qs, hw)) for _ in range(2)],
        vm((slots, wide)),
        *[vm((n_grp // 2, feats, toks)) for _ in range(3)],
        *[vm((2, half, feats, toks)) for _ in range(2)],
        sem(2, half, ZP), sem(2, half, ZP), sem(2, half + 1), sem(2, half + 1),
        sem(6, 2, 2, 3), sem(6, 2, 2, 3),
        sem(2, half, RP), sem(2, half, RP), sem(n_grp // 2), sem(n_grp // 2),
    ]
    whole = pl.BlockSpec(memory_space=pltpu.VMEM)
    down_t, input_t = pl.pallas_call(
        moe_kernel,
        out_shape=(
            jax.ShapeDtypeStruct((feats, hidden), BF16),
            jax.ShapeDtypeStruct((feats, toks), BF16),
        ),
        in_specs=[whole] * 7,
        out_specs=(whole, whole),
        scratch_shapes=scratch,
        compiler_params=pltpu.CompilerParams(
            collective_id=0, has_side_effects=True, vmem_limit_bytes=58 * 1024 * 1024
        ),
    )(
        out_grad.T,
        group_choice.T,
        gate_weight.transpose(1, 2, 0).reshape(picks * experts, toks),
        gate_pre[0],
        up_pre[0],
        down_weight[0].T,
        up_weight[0].T,
    )
    return down_t.T[None], input_t.T


def solution(mesh):
    return jax.shard_map(
        on_device,
        mesh=mesh,
        in_specs=(
            P("grp", "loc"),
            P("grp", None),
            P("grp", None, None),
            P("grp", None, "loc"),
            P("grp", None, "loc"),
            P("grp", None, "loc"),
            P("grp", None, "loc"),
        ),
        out_specs=(P("grp", None, "loc"), P("grp", "loc")),
        check_vma=False,
    )
```

time: 435 us -> 194 us (0.45)
  waiting for transfers between devices: 332 us -> 0 us
  Pallas kernels: 0 us -> 187 us
  starting transfers between devices: 60 us -> 0 us
  between operations: 13.9 us -> 0.65 us
  matrix products: 13.2 us -> 0 us
  local copies, waits for them, and re-layouts: 10 us -> 2.84 us
  other arithmetic: 5.06 us -> 0 us
    pallas_call x0 -> x1, Pallas kernels: none -> 187 us  [on_device(): pl.pallas_call(moe_kernel, out_shape=(jax.ShapeDtypeStruct((feats, hidden...]
    all_gather x2 -> x0, waiting for transfers between devices: 155 us -> none  [the longest x1 91.5 us: on_device(): lax.all_gather(up_grad, 'loc', axis=1, tiled=True)]
    reduce_scatter x1 -> x0, waiting for transfers between devices: 92.9 us -> none  [on_device(): lax.psum_scatter(partial_value.astype(jnp.bfloat16), 'loc', scatter_dimen...]
    all_to_all x3 -> x0, waiting for transfers between devices: 83.3 us -> none  [the longest x1 62.5 us: on_device(): lax.all_to_all(outgoing.reshape(group_count, capacity, feature_count), 'g...]
    all_to_all x3 -> x0, starting transfers between devices: 59.8 us -> none  [the longest x1 30.4 us: on_device(): lax.all_to_all(outgoing_gate.reshape(group_count, capacity, expert_count)...]
    dot_general x6 -> x0, matrix products: 13.2 us -> none  [the longest x1 4.48 us: on_device(): jnp.einsum('red,efd->ref', weighted_bf, down_block, preferred_element_typ...]
  transfers between devices with their start and end apart: 6 -> 0, of which waited for: 5 -> 0; matrix products, arithmetic and copies ran while one was open for 3% -> 0% of each run, Pallas kernels for 0% -> 0%
where the time goes in v1:
time: 194 us; the launch traced here: 191 us
  Pallas kernels  187 us (96%)
  local copies, waits for them, and re-layouts  2.84 us (1%)
    pallas_call x1, Pallas kernels, on_device(): pl.pallas_call(moe_kernel, out_shape=(jax.ShapeDtypeStruct((feats, hidden...  187 us

profile of v1, /device:TPU:1, one launch (start us, length us, event | category | flops | bytes accessed | tf_op | source)
XLA Modules:
  0.0 190.9 jit_solution(5378251141635062566)
XLA Ops:
  0.6 187.4 %shard_map.86 = (bf16[224,2048]{1,0:T(8,128)(2,1)}, bf16[224,128]{1,0:T(8,128)(2,1)}) custom-call(bf16[224,128]{1,0:T(8,128)(2,1)} %bitcast.23, s32[4,128]{1,0:T(4,128)} %bitcast.24, bf16[8,128]{1,0:T(8,128)(2,1)} %bitcast.25, bf16[1024,128]{1,0:T(8,128)(2,1)} %bitcast.20, bf16[1024,128]{1,0:T(8,128)(2,1)} %bitcast.21, bf16[224,2048]{1,0:T(8,128)(2,1)} %bitcast.18, ...), custom_call_target="tpu_custom_call" | custom-call | tf_op jit(solution)/shard_map/pallas_call | solution.py:519
  188.1 0.0 copy-start
  188.1 2.2 %copy.11 = bf16[1,2048,224]{1,2,0:T(8,128)(2,1)} copy(bf16[1,2048,224]{1,2,0:T(8,128)(2,1)} %bitcast.17) | data formatting | bytes 1835008
  190.3 0.0 copy-done
  190.3 0.6 copy.12
Async XLA Ops:
  188.1 2.2 %copy-start = (bf16[224,128]{1,0:T(8,128)(2,1)S(1)}, bf16[224,128]{1,0:T(8,128)(2,1)}, u32[]{:S(2)}) copy-start(bf16[224,128]{1,0:T(8,128)(2,1)} %get-tuple-element.5) | copy-start | bytes 172036

commit v2 on v1

--- a/solution.py
+++ b/solution.py
@@ -12,8 +12,9 @@
 TN = (((0,), (0,)), ((), ()))
 F32 = jnp.float32
 BF16 = jnp.bfloat16
-ZP = 3
-RP = 2
+JUMP = 2
+OUT = 3
+BACK = 2
 
 
 def moe_kernel(
@@ -57,7 +58,9 @@
         )
 
     barrier = pltpu.get_barrier_semaphore()
-    for dev in zdev + [sib] + xdev + ydev:
+    far = [(gz(r) * 2 + c, loc) for j in range(2, JUMP + 1) for r in (j, -j)]
+    greeted = zdev + far + [sib] + xdev + ydev
+    for dev in greeted:
         pl.semaphore_signal(barrier, inc=1, device_id=dev, device_id_type=MESH)
 
     choice = choice_ref[...].astype(F32)
@@ -78,20 +81,26 @@
     allx[g, 0:feats, :] = x_ref[...]
     allx[g, feats:, :] = meta.astype(BF16)
 
-    pl.semaphore_wait(barrier, 7)
-
-    zrows = allx.shape[1] // ZP
+    pl.semaphore_wait(barrier, len(greeted))
+
 
     def blk(r):
         return gz(r) * 2 + c
 
-    def zcopy(d, s, p):
-        ref = allx.at[blk(-s if d == 0 else s), pl.ds(p * zrows, zrows), :]
-        return copy(ref, ref, zsend.at[d, s, p], zrecv.at[d, s, p], zdev[d])
-
-    def zwait(d, s, p):
-        ref = allx.at[blk(-(s + 1) if d == 0 else s + 1), pl.ds(p * zrows, zrows), :]
-        copy(ref, ref, zsend.at[d, s, p], zrecv.at[d, s, p], zdev[d]).wait_recv()
+    def base(d):
+        return (d - 1) // JUMP * JUMP if isinstance(d, int) else lax.div(d - 1, JUMP) * JUMP
+
+    zrows = allx.shape[1] // OUT
+
+    def zcopy(w, d, p):
+        b = base(d)
+        ref = allx.at[blk(-b if w == 0 else b), pl.ds(p * zrows, zrows), :]
+        dev = (blk(d - b if w == 0 else b - d), loc)
+        return copy(ref, ref, zsend.at[w, d - 1, p], zrecv.at[w, d - 1, p], dev)
+
+    def zwait(w, d, p):
+        ref = allx.at[blk(-d if w == 0 else d), pl.ds(p * zrows, zrows), :]
+        copy(ref, ref, zsend.at[w, d - 1, p], zrecv.at[w, d - 1, p], zdev[w]).wait_recv()
 
     def bcopy(d, s):
         ref = allx.at[blk(-s if d == 0 else s)]
@@ -124,32 +133,45 @@
             wf[e, at, 0:feats] = w[e * cap : (e + 1) * cap]
             wbf[e, at, 0:feats] = w[e * cap : (e + 1) * cap].astype(BF16)
 
-    def zstep(s, up=True, down=True, lag=True):
-        for p in range(ZP):
-            zwait(0, s - 1, p)
-            if up:
-                zcopy(0, s, p).start()
-            if down is not None:
-                zwait(1, s - 1, p)
-                if down:
-                    zcopy(1, s, p).start()
-        bcopy(0, s).start()
-        build(blk(-s))
-        if down is not None:
-            bcopy(1, s).start()
-            build(blk(s))
-        if lag:
-            for d in range(2):
-                bwait(d, s - 1)
-                build(gz(-(s - 1) if d == 0 else s - 1) * 2 + 1 - c)
-
-    def zloop(lo, hi):
-        lo, hi = min(lo, half - 1), min(hi, half - 1)
-        if lo < hi:
-            def step(s, carry):
-                zstep(s)
-                return carry
-            lax.fori_loop(lo, hi, step, 0)
+    def zpass(k):
+        for p in range(OUT):
+            for w in range(2):
+                if 0 < k * JUMP <= half - w:
+                    zwait(w, k * JUMP, p)
+                if (k + 1) * JUMP <= half - w:
+                    zcopy(w, (k + 1) * JUMP, p).start()
+        for j in range(1, JUMP):
+            for p in range(OUT):
+                for w in range(2):
+                    if k * JUMP + j <= half - w:
+                        zcopy(w, k * JUMP + j, p).start()
+
+    def landed(d, ways):
+        for w in ways:
+            bcopy(w, d).start()
+        for w in ways:
+            build(blk(-d if w == 0 else d))
+
+    def crossed(d, ways):
+        for w in ways:
+            bwait(w, d)
+            build(gz(-d if w == 0 else d) * 2 + 1 - c)
+
+    def spread(lo, hi, what):
+        def step(d, carry):
+            what(d, (0, 1))
+            return carry
+
+        if lo < min(hi, half):
+            lax.fori_loop(lo, min(hi, half), step, 0)
+        if lo <= half < hi:
+            what(half, (0,))
+
+    def filled(d, ways):
+        for p in range(OUT):
+            for w in ways:
+                zwait(w, d, p)
+        landed(d, ways)
 
     def ring(stage, h):
         a = (pos1 if stage in (0, 3, 5) else pos2)[h]
@@ -234,9 +256,7 @@
     def own_rows(h, k):
         return (pos1[h], lax.div(pos2[h], 2), pl.ds(pl.multiple_of(lax.rem(pos2[h], 2) * hs + k * qs, qs), qs))
 
-    for p in range(ZP):
-        for d in range(2):
-            zcopy(d, 0, p).start()
+    zpass(0)
     bcopy(0, 0).start()
 
     for h in range(2):
@@ -253,23 +273,31 @@
     bwait(0, 0)
     build(z * 2 + 1 - c)
 
-    zstep(1, down=half > 2, lag=False)
-    zloop(2, 4)
-    for h in range(2):
-        ag_pass(2, gh, h)
-    zloop(4, 6)
-    for h in range(2):
-        ag_finish(2, gh, h)
-        ag_send(3, gh, h)
-    zloop(6, 12)
-    for h in range(2):
-        ag_pass(3, gh, h)
-    zloop(12, half - 1)
-    if half > 2:
-        zstep(half - 1, down=False)
-    zstep(half, up=False, down=None)
-    bwait(0, half)
-    build(gz(-half) * 2 + 1 - c)
+    def early(k):
+        if k == 1:
+            for h in range(2):
+                ag_pass(2, gh, h)
+        if k == 2:
+            for h in range(2):
+                ag_finish(2, gh, h)
+                ag_send(3, gh, h)
+        if k == 4:
+            for h in range(2):
+                ag_pass(3, gh, h)
+
+    tops = half // JUMP
+    for k in range(1, tops + 1):
+        ways = (0, 1) if k * JUMP < half else (0,)
+        zpass(k)
+        landed(k * JUMP, ways)
+        spread((k - 1) * JUMP + 1, k * JUMP, filled)
+        early(k)
+        if k > 1:
+            spread((k - 2) * JUMP + 1, (k - 1) * JUMP + 1, crossed)
+    spread(tops * JUMP + 1, half + 1, filled)
+    for k in range(tops + 1, 5):
+        early(k)
+    spread((tops - 1) * JUMP + 1, half + 1, crossed)
 
     def partial(h, t):
         def step(q, carry):
@@ -389,7 +417,6 @@
 
         lax.fori_loop(0, 2, back, 0)
 
-    rrows = feats // RP
 
     def contrib(n):
         zt = gz(n)
@@ -414,53 +441,75 @@
     def cwait(n):
         copy(sibs.at[n], sibr.at[n], csend.at[n], crecv.at[n], sib).wait_recv()
 
-    def index(d, s):
-        return half - s if d == 0 else lax.rem(half + 1 + s, n_z)
-
-    def rcopy(d, s, p):
+    def index(w, d):
+        return d if w == 0 else lax.rem(n_z - d, n_z)
+
+    rrows = feats // BACK
+
+    def rcopy(w, d, p):
+        b = base(d)
+        dev = (blk(d - b if w == 0 else b - d), loc)
         at = pl.ds(p * rrows, rrows)
-        return copy(rings.at[d, s, at, :], ringr.at[d, s, at, :], rsend.at[d, s, p], rrecv.at[d, s, p], zdev[d])
-
-    def rstep(s, first=False, both=True):
-        dirs = (0, 1) if both else (0,)
-        for d in dirs:
-            cwait(index(d, s))
-        for p in range(RP):
-            at = slice(p * rrows, (p + 1) * rrows)
-            for d in dirs:
-                n = index(d, s)
-                total = own[n, at, :].astype(F32) + sibr[n, at, :].astype(F32)
-                if not first:
-                    rcopy(d, s - 1, p).wait_recv()
-                    total += ringr[d, s - 1, at, :].astype(F32)
-                rings[d, s, at, :] = total.astype(BF16)
-                rcopy(d, s, p).start()
-
-    contrib(index(0, 0))
-    contrib(index(1, 0))
-    contrib(index(0, 1))
-    contrib(index(1, 1))
-    rstep(0, first=True)
-
-    def rloop(s, carry):
-        contrib(index(0, s + 1))
-        contrib(index(1, s + 1))
-        rstep(s)
-        return carry
-
-    lax.fori_loop(1, half - 1, rloop, 0)
-    rstep(half - 1, both=False)
+        return copy(
+            rings.at[w, d - 1, at, :], ringr.at[w, d - 1, at, :], rsend.at[w, d - 1, p], rrecv.at[w, d - 1, p], dev
+        )
+
+    def here(n, p):
+        at = pl.ds(p * rrows, rrows)
+        return own[n, at, :].astype(F32) + sibr[n, at, :].astype(F32)
+
+    def came(w, d, p):
+        total = jnp.zeros((rrows, toks), F32)
+        for j in range(1, JUMP + 1):
+            if d + j <= half - w:
+                rcopy(w, d + j, p).wait_recv()
+                total += ringr[w, d + j - 1, pl.ds(p * rrows, rrows), :].astype(F32)
+        return total
+
+    def add(d, ways):
+        for w in ways:
+            contrib(index(w, d))
+
+    def adds(k):
+        if k == 0:
+            contrib(0)
+        spread(max(k * JUMP, 1), k * JUMP + JUMP if k < tops else half + 1, add)
+
+    def leaf(d, ways):
+        for w in ways:
+            cwait(index(w, d))
+        for p in range(BACK):
+            for w in ways:
+                rings[w, d - 1, pl.ds(p * rrows, rrows), :] = here(index(w, d), p).astype(BF16)
+                rcopy(w, d, p).start()
+
+    def leaves(k):
+        spread(k * JUMP + 1, k * JUMP + JUMP if k < tops else half + 1, leaf)
+
+    def lead(k):
+        d = k * JUMP
+        ways = (0, 1) if d < half else (0,)
+        for w in ways:
+            cwait(index(w, d))
+        for p in range(BACK):
+            for w in ways:
+                total = here(index(w, d), p) + came(w, d, p)
+                rings[w, d - 1, pl.ds(p * rrows, rrows), :] = total.astype(BF16)
+                rcopy(w, d, p).start()
+
+    for k in (tops, tops - 1):
+        adds(k)
+        leaves(k)
+    for k in range(tops, 0, -1):
+        if k > 1:
+            adds(k - 2)
+        lead(k)
+        if k > 1:
+            leaves(k - 2)
     cwait(0)
-    for p in range(RP):
-        at = slice(p * rrows, (p + 1) * rrows)
-        rcopy(0, half - 1, p).wait_recv()
-        rcopy(1, half - 2, p).wait_recv()
-        ig_ref[at, :] = (
-            own[0, at, :].astype(F32)
-            + sibr[0, at, :].astype(F32)
-            + ringr[0, half - 1, at, :].astype(F32)
-            + ringr[1, half - 2, at, :].astype(F32)
-        ).astype(BF16)
+    for p in range(BACK):
+        total = here(0, p) + came(0, 0, p) + came(1, 0, p)
+        ig_ref[pl.ds(p * rrows, rrows), :] = total.astype(BF16)
 
     def drain(lo, hi, what):
         def step(s, carry):
@@ -468,11 +517,11 @@
             return carry
         lax.fori_loop(lo, hi, step, 0)
 
-    for d in range(2):
-        for p in range(ZP):
-            drain(0, half - d, lambda s: zcopy(d, s, p).wait_send())
-        for p in range(RP):
-            drain(0, half - d, lambda s: rcopy(d, s, p).wait_send())
+    for w in range(2):
+        for p in range(OUT):
+            drain(1, half + 1 - w, lambda d: zcopy(w, d, p).wait_send())
+        for p in range(BACK):
+            drain(1, half + 1 - w, lambda d: rcopy(w, d, p).wait_send())
     drain(0, half + 1, lambda s: bcopy(0, s).wait_send())
     drain(1, half, lambda s: bcopy(1, s).wait_send())
     drain(0, n_z, lambda n: copy(sibs.at[n], sibr.at[n], csend.at[n], crecv.at[n], sib).wait_send())
@@ -511,9 +560,9 @@
         vm((slots, wide)),
         *[vm((n_grp // 2, feats, toks)) for _ in range(3)],
         *[vm((2, half, feats, toks)) for _ in range(2)],
-        sem(2, half, ZP), sem(2, half, ZP), sem(2, half + 1), sem(2, half + 1),
+        sem(2, half, OUT), sem(2, half, OUT), sem(2, half + 1), sem(2, half + 1),
         sem(6, 2, 2, 3), sem(6, 2, 2, 3),
-        sem(2, half, RP), sem(2, half, RP), sem(n_grp // 2), sem(n_grp // 2),
+        sem(2, half, BACK), sem(2, half, BACK), sem(n_grp // 2), sem(n_grp // 2),
     ]
     whole = pl.BlockSpec(memory_space=pltpu.VMEM)
     down_t, input_t = pl.pallas_call(

time: 194 us -> 166 us (0.86)
  Pallas kernels: 187 us -> 159 us
    pallas_call x1, Pallas kernels: 187 us -> 159 us  [on_device(): pl.pallas_call(moe_kernel, out_shape=(jax.ShapeDtypeStruct((feats, hidden...]
where the time goes in v2:
time: 166 us; the launch traced here: 163 us
  Pallas kernels  159 us (96%)
  local copies, waits for them, and re-layouts  2.84 us (2%)
    pallas_call x1, Pallas kernels, on_device(): pl.pallas_call(moe_kernel, out_shape=(jax.ShapeDtypeStruct((feats, hidden...  159 us

profile of v2, /device:TPU:1, one launch (start us, length us, event | category | flops | bytes accessed | tf_op | source)
XLA Modules:
  0.0 162.7 jit_solution(4076275603131867259)
XLA Ops:
  0.6 159.2 %shard_map.86 = (bf16[224,2048]{1,0:T(8,128)(2,1)}, bf16[224,128]{1,0:T(8,128)(2,1)}) custom-call(bf16[224,128]{1,0:T(8,128)(2,1)} %bitcast.23, s32[4,128]{1,0:T(4,128)} %bitcast.24, bf16[8,128]{1,0:T(8,128)(2,1)} %bitcast.25, bf16[1024,128]{1,0:T(8,128)(2,1)} %bitcast.20, bf16[1024,128]{1,0:T(8,128)(2,1)} %bitcast.21, bf16[224,2048]{1,0:T(8,128)(2,1)} %bitcast.18, ...), custom_call_target="tpu_custom_call" | custom-call | tf_op jit(solution)/shard_map/pallas_call | solution.py:568
  159.9 0.0 copy-start
  159.9 2.2 %copy.11 = bf16[1,2048,224]{1,2,0:T(8,128)(2,1)} copy(bf16[1,2048,224]{1,2,0:T(8,128)(2,1)} %bitcast.17) | data formatting | bytes 1835008
  162.1 0.0 copy-done
  162.1 0.6 copy.12
Async XLA Ops:
  159.9 2.2 %copy-start = (bf16[224,128]{1,0:T(8,128)(2,1)S(1)}, bf16[224,128]{1,0:T(8,128)(2,1)}, u32[]{:S(2)}) copy-start(bf16[224,128]{1,0:T(8,128)(2,1)} %get-tuple-element.5) | copy-start | bytes 172036
